TPU v7x, 512 devices: a whole 4x4x16 slice. The times are simulated.
512 devices in a mesh: tile: 64 (over z, x_lo, core), tensor: 8 (over x_hi, y).
Axes of the slice: x: 4 (x_hi: 2, x_lo: 2; x = x_hi * 2 + x_lo), y: 4, z: 16, core: 2. Of those that a mesh axis runs over, the one named last changes fastest.
Arguments:
- tokens: bfloat16 [16384, 4096], P('tile'), may hold values from -6 to 6
- w_qkv: bfloat16 [3, 4096, 2048], P(None, 'tile', 'tensor'), may hold values from -0.09375 to 0.09375
- w_out: bfloat16 [2048, 4096], P('tensor', 'tile'), may hold values from -0.25 to 0.25
- window_ext: int32 [16, 3], P('tensor'), may hold values from 0 to 8, as said below
Outputs:
- mixed: bfloat16 [16384, 4096], P('tile', 'tensor')
Inputs may be any that keep to these rules, and one draw needn't show every extreme that they name: `window_ext`: column 0 is at most 2, columns 1 and 2 lie from 1 to 4 and 1 to 8; each column's largest allowed value is taken by some head.
All inputs are finite; a program needn't handle non-finite values.
Results may differ from a plain program's by a relative error of at most 0.017.
Values may be sent and summed in bfloat16 or wider, within the bound.
A program may use at most 64 MiB of HBM per device.

v0:
```python
import jax
import jax.numpy as jnp
from jax import lax
from jax.sharding import PartitionSpec as P

HD = 128
TT = 2
TH = 8
TW = 16
GH = 4
GW = 4


def from_behind(shard, axis, by):
    devices = lax.axis_size(axis)
    pairs = [(i, i + by) for i in range(devices) if 0 <= i + by < devices]
    return lax.ppermute(shard, axis, pairs)


def unit_rows(proj, heads_here):
    heads = proj.reshape(proj.shape[0], heads_here, HD)
    scale = lax.rsqrt(jnp.mean(heads * heads, axis=-1, keepdims=True) + 1e-06)
    return (heads * scale).astype(jnp.bfloat16)


def edge_rows(values, by):
    return from_behind(values, "tile", by)


def side_piece(values, by):
    return from_behind(values, "tile", by)


def side_cols(values):
    reach_w = TW // 2
    left = side_piece(values[:, :, TW - reach_w :], 1)
    right = side_piece(values[:, :, :reach_w], -1)
    return jnp.concatenate([left, values, right], axis=2)


def grid_coords(shape):
    first = jnp.arange(shape[0], dtype=jnp.int32)[:, None, None] + jnp.zeros(shape, jnp.int32)
    second = jnp.arange(shape[1], dtype=jnp.int32)[None, :, None] + jnp.zeros(shape, jnp.int32)
    third = jnp.arange(shape[2], dtype=jnp.int32)[None, None, :] + jnp.zeros(shape, jnp.int32)
    return (first.reshape(-1), second.reshape(-1), third.reshape(-1))


def per_device(tokens, w_qkv, w_out, window_ext):
    tok_rows = tokens.shape[0]
    head_cols = w_qkv.shape[2]
    heads_here = head_cols // HD
    reach_t = TT
    reach_h = TH // 2
    reach_w = TW // 2
    proj = jnp.einsum(
        "tn,jnc->jtc",
        tokens,
        lax.all_gather(w_qkv, "tile", axis=1, tiled=True),
        preferred_element_type=jnp.float32,
    )
    query = unit_rows(proj[0], heads_here)
    key = unit_rows(proj[1], heads_here)
    value = proj[2].astype(jnp.bfloat16)
    paired = jnp.concatenate([key.reshape(tok_rows, head_cols), value], axis=1)
    paired = paired.reshape(TT, TH, TW, 2 * head_cols)
    region = side_cols(paired)
    region = jnp.concatenate(
        [edge_rows(region[:, TH - reach_h :], GW), region, edge_rows(region[:, :reach_h], -GW)],
        axis=1,
    )
    region = jnp.concatenate([edge_rows(region, GH * GW), region], axis=0)
    kshape = (TT + reach_t, TH + 2 * reach_h, TW + 2 * reach_w)
    n_keys = kshape[0] * kshape[1] * kshape[2]
    region = region.reshape(n_keys, 2 * head_cols)
    keys = region[:, :head_cols].reshape(n_keys, heads_here, HD)
    vals = region[:, head_cols:].reshape(n_keys, heads_here, HD)
    index = lax.axis_index("tile")
    tile_t = index // (GH * GW)
    tile_h = index // GW % GH
    tile_w = index % GW
    rows_all = GH * TH
    cols_all = GW * TW
    qa, qb, qc = grid_coords((TT, TH, TW))
    ka, kb, kc = grid_coords(kshape)
    q_f = tile_t * TT + qa
    q_r = tile_h * TH + qb
    q_c = tile_w * TW + qc
    k_f = tile_t * TT - reach_t + ka
    k_r = tile_h * TH - reach_h + kb
    k_c = tile_w * TW - reach_w + kc
    inside = (k_f >= 0) & (k_r >= 0) & (k_r < rows_all) & (k_c >= 0) & (k_c < cols_all)
    d_f = q_f[:, None] - k_f[None, :]
    d_r = jnp.abs(q_r[:, None] - k_r[None, :])
    d_c = jnp.abs(q_c[:, None] - k_c[None, :])
    seen = (d_f[None] >= 0) & (d_f[None] <= window_ext[:, 0, None, None])
    seen = (
        seen
        & (d_r[None] <= window_ext[:, 1, None, None])
        & (d_c[None] <= window_ext[:, 2, None, None])
    )
    seen = seen & inside[None, None, :]
    scores = jnp.einsum("qhd,khd->hqk", query, keys, preferred_element_type=jnp.float32) / jnp.sqrt(
        jnp.float32(HD)
    )
    weight = jnp.where(seen, jnp.exp(scores), jnp.float32(0.0))
    total = jnp.sum(weight, axis=-1)
    weight_b = weight.astype(jnp.bfloat16)
    summed = jnp.einsum("hqk,khd->qhd", weight_b, vals, preferred_element_type=jnp.float32)
    attended = (
        (summed / jnp.transpose(total)[:, :, None])
        .astype(jnp.bfloat16)
        .reshape(tok_rows, head_cols)
    )
    terms = jnp.dot(
        attended,
        lax.all_gather(w_out, "tile", axis=1, tiled=True),
        preferred_element_type=jnp.float32,
    )
    return lax.psum_scatter(terms.astype(jnp.bfloat16), "tensor", scatter_dimension=1, tiled=True)


def solution(mesh):
    in_specs = (P("tile", None), P(None, "tile", "tensor"), P("tensor", "tile"), P("tensor", None))
    out_specs = P("tile", "tensor")
    return jax.shard_map(
        per_device, mesh=mesh, in_specs=in_specs, out_specs=out_specs, check_vma=False
    )
```

profile of v0, /device:TPU:32, one launch (start us, length us, event | category | flops | bytes accessed | tf_op | source)
XLA Modules:
  0.0 429.7 jit_solution(6686151900206497320)
XLA Ops:
  6.5 0.0 copy-start
  6.5 0.0 all-gather.3.cloned.1.call-start
  6.5 0.7 all-gather.3.cloned.1.call-update
  7.3 0.0 all-gather.5.cloned.1.call-start
  7.3 0.7 all-gather.5.cloned.1.call-update
  8.0 0.0 reduce-scatter.2.cloned.1.call-start
  8.1 0.1 add.158
  8.2 0.1 add.154
  8.3 1.6 broadcast_subtract_fusion
  9.8 1.2 broadcast_compare_fusion
  11.0 129.8 %all-gather.3.cloned.1.call-done = bf16[3,4096,256]{2,1,0:T(8,128)(2,1)} async-done(((bf16[3,64,256]{2,1,0:T(8,128)(2,1)}), bf16[3,4096,256]{2,1,0:T(8,128)(2,1)}) %all-gather.3.cloned.1.call-update) | async-done | bytes 6291472 | tf_op jit(solution)/shard_map/all_gather | solution.py:58
  140.8 4.6 %fusion.4 = f32[3,256,256]{1,2,0:T(8,128)S(1)} fusion(bf16[3,4096,256]{2,1,0:T(8,128)(2,1)} %all-gather.3.cloned.1.call-done, bf16[256,4096]{1,0:T(8,128)(2,1)S(1)} %copy-done), kind=kOutput, calls=%fused_computation.9 | convolution fusion | flops 1610612736 | bytes 9175040 | tf_op jit(solution)/shard_map/tn,jnc->jtc/dot_general | solution.py:55
  145.4 0.1 fusion.19
  145.5 0.1 copy.13
  145.7 0.1 copy.14
  145.9 0.3 mul.51
  146.2 0.2 mul.52
  146.4 0.1 copy.15
  146.6 2.7 collective-permute-start.1
  149.3 1.9 collective-permute-start
  151.3 0.0 copy-start.2
  151.3 0.5 collective-permute-done.1
  151.8 4.7 %collective-permute-done = bf16[2,8,8,512]{3,2,1,0:T(8,128)(2,1)S(1)} collective-permute-done((bf16[2,8,8,512]{3,2,1,0:T(8,128)(2,1)S(1)}, bf16[2,8,8,512]{3,2,1,0:T(8,128)(2,1)S(1)}, u32[]{:S(2)}, u32[]{:S(2)}) %collective-permute-start) | collective-permute-done | bytes 131104 | tf_op jit(solution)/shard_map/ppermute | solution.py:17
  156.6 0.8 fusion.20
  157.4 1.9 collective-permute-start.3
  159.3 4.0 collective-permute-start.2
  163.3 0.1 add.176
  163.4 0.1 add.167
  163.5 3.1 collective-permute-done.3
  166.6 2.0 collective-permute-done.2
  168.6 1.1 pad_maximum_fusion
  169.7 9.2 %collective-permute-start.4 = (bf16[2,16,32,512]{3,2,1,0:T(8,128)(2,1)}, bf16[2,16,32,512]{3,2,1,0:T(8,128)(2,1)}, u32[]{:S(2)}, u32[]{:S(2)}) collective-permute-start(bf16[2,16,32,512]{3,2,1,0:T(8,128)(2,1)} %pad_maximum_fusion), channel_id=1, source_target_pairs={{0,128},{8,136},{16,144},{24,152},{32,160},{40,168},{48,176},{56,1... | collective-permute-start | bytes 3145736 | tf_op jit(solution)/shard_map/ppermute | solution.py:17
  178.9 0.1 add.172
  179.0 0.1 add.163
  179.1 0.2 slice_reduce_fusion.2
  179.2 2.6 subtract_abs_fusion
  181.9 37.9 %collective-permute-done.4 = bf16[2,16,32,512]{3,2,1,0:T(8,128)(2,1)} collective-permute-done((bf16[2,16,32,512]{3,2,1,0:T(8,128)(2,1)}, bf16[2,16,32,512]{3,2,1,0:T(8,128)(2,1)}, u32[]{:S(2)}, u32[]{:S(2)}) %collective-permute-start.4) | collective-permute-done | bytes 1048608 | tf_op jit(solution)/shard_map/ppermute | solution.py:17
  219.8 1.4 maximum_maximum_fusion
  221.2 1.1 fusion.18
  222.3 2.3 copy.16
  224.6 1.4 copy.17
  226.0 5.7 %fusion.21 = (f32[2,256]{1,0:T(2,128)S(1)}, bf16[2,256,2048]{2,1,0:T(8,128)(2,1)S(1)}) fusion(bf16[2048,2,128]{0,2,1:T(8,128)(2,1)} %bitcast.37, f32[256,2,128]{0,2,1:T(8,128)S(1)} %bitcast.34, f32[256,2]{0,1:T(2,128)S(1)} %add_rsqrt_fusion, pred[2048]{0:T(1024)(128)(4,1)S(1)} %compare_and_fusion, s32[2]{0:T(128)S(1)} %get-tuple-element.6, ...), kind=kOutput, calls=%fused_computation.42 | convolution fusion | flops 280100352 | bytes 10229784 | tf_op jit(solution)/shard_map/qhd,khd->hqk/dot_general | solution.py:102
  231.7 0.0 copy-done.1
  231.7 0.8 fusion.13
  232.6 96.7 %all-gather.5.cloned.1.call-done = bf16[256,4096]{0,1:T(8,128)(2,1)} async-done(((bf16[256,64]{0,1:T(8,128)(2,1)}), bf16[256,4096]{0,1:T(8,128)(2,1)}) %all-gather.5.cloned.1.call-update) | async-done | bytes 2097168 | tf_op jit(solution)/shard_map/all_gather | solution.py:116
  329.3 3.7 convolution_convert_fusion
  332.9 0.0 reduce-scatter.2.cloned.1.call-update
  333.0 90.2 %reduce-scatter.2.cloned.1.call-done = bf16[256,512]{1,0:T(8,128)(2,1)} async-done(((bf16[256,4096]{1,0:T(8,128)(2,1)}), bf16[256,512]{1,0:T(8,128)(2,1)}) %reduce-scatter.2.cloned.1.call-update) | async-done | bytes 262160 | tf_op jit(solution)/shard_map/reduce_scatter | solution.py:119
  (18 shorter events, 0.3 us)
Async XLA Ops:
  6.5 134.3 %copy-start = (bf16[256,4096]{1,0:T(8,128)(2,1)S(1)}, bf16[256,4096]{1,0:T(8,128)(2,1)}, u32[]{:S(2)}) copy-start(bf16[256,4096]{1,0:T(8,128)(2,1)} %param.4) | copy-start | bytes 6291460
  6.5 134.3 %all-gather.3.cloned.1.call-start = ((), (), s32[]{:S(2)}) async-start(), calls=%async_computation.1 | async-start | bytes 6389760 | tf_op jit(solution)/shard_map/all_gather | solution.py:58
  7.3 322.0 %all-gather.5.cloned.1.call-start = ((), (), s32[]{:S(2)}) async-start(), calls=%async_computation.2 | async-start | bytes 2129920 | tf_op jit(solution)/shard_map/all_gather | solution.py:116
  8.0 415.2 %reduce-scatter.2.cloned.1.call-start = ((), (), s32[]{:S(2)}) async-start(), calls=%async_computation.3 | async-start | bytes 2359296 | tf_op jit(solution)/shard_map/reduce_scatter | solution.py:119
  146.6 5.2 %collective-permute-start.1 = (bf16[2,8,8,512]{3,2,1,0:T(8,128)(2,1)S(1)}, bf16[2,8,8,512]{3,2,1,0:T(8,128)(2,1)S(1)}, u32[]{:S(2)}, u32[]{:S(2)}) collective-permute-start(bf16[2,8,8,512]{3,2,1,0:T(8,128)(2,1)S(1)} %get-tuple-element.16), channel_id=1, source_target_pairs={{8,0},{16,8},{24,16},{32,24},{40,32},{48,40},{56,48},{64,56},{72,6... | collective-permute-start | bytes 393224 | tf_op jit(solution)/shard_map/ppermute | solution.py:17
  149.3 7.2 %collective-permute-start = (bf16[2,8,8,512]{3,2,1,0:T(8,128)(2,1)S(1)}, bf16[2,8,8,512]{3,2,1,0:T(8,128)(2,1)S(1)}, u32[]{:S(2)}, u32[]{:S(2)}) collective-permute-start(bf16[2,8,8,512]{3,2,1,0:T(8,128)(2,1)S(1)} %get-tuple-element.15), channel_id=1, source_target_pairs={{0,8},{8,16},{16,24},{24,32},{32,40},{40,48},{48,56},{56,64},{64,7... | collective-permute-start | bytes 393224 | tf_op jit(solution)/shard_map/ppermute | solution.py:17
  151.3 27.7 %copy-start.2 = (s32[2,3]{1,0:T(2,128)S(1)}, s32[2,3]{1,0:T(2,128)}, u32[]{:S(2)}) copy-start(s32[2,3]{1,0:T(2,128)} %param.7) | copy-start | bytes 76
  157.4 9.2 %collective-permute-start.3 = (bf16[2,4,32,512]{3,2,1,0:T(8,128)(2,1)}, bf16[2,4,32,512]{3,2,1,0:T(8,128)(2,1)S(1)}, u32[]{:S(2)}, u32[]{:S(2)}) collective-permute-start(bf16[2,4,32,512]{3,2,1,0:T(8,128)(2,1)} %get-tuple-element.14), channel_id=1, source_target_pairs={{32,0},{40,8},{48,16},{56,24},{64,32},{72,40},{80,48},{88,56},{96,... | collective-permute-start | bytes 786440 | tf_op jit(solution)/shard_map/ppermute | solution.py:17
  159.3 9.3 %collective-permute-start.2 = (bf16[2,4,32,512]{3,2,1,0:T(8,128)(2,1)}, bf16[2,4,32,512]{3,2,1,0:T(8,128)(2,1)S(1)}, u32[]{:S(2)}, u32[]{:S(2)}) collective-permute-start(bf16[2,4,32,512]{3,2,1,0:T(8,128)(2,1)} %get-tuple-element.13), channel_id=1, source_target_pairs={{0,32},{8,40},{16,48},{24,56},{32,64},{40,72},{48,80},{56,88},{64,... | collective-permute-start | bytes 786440 | tf_op jit(solution)/shard_map/ppermute | solution.py:17
  169.7 50.1 %collective-permute-start.4 = (bf16[2,16,32,512]{3,2,1,0:T(8,128)(2,1)}, bf16[2,16,32,512]{3,2,1,0:T(8,128)(2,1)}, u32[]{:S(2)}, u32[]{:S(2)}) collective-permute-start(bf16[2,16,32,512]{3,2,1,0:T(8,128)(2,1)} %pad_maximum_fusion), channel_id=1, source_target_pairs={{0,128},{8,136},{16,144},{24,152},{32,160},{40,168},{48,176},{56,1... | collective-permute-start | bytes 3145736 | tf_op jit(solution)/shard_map/ppermute | solution.py:17
  226.0 5.7 %copy-start.1 = (bf16[2048,256]{0,1:T(8,128)(2,1)S(1)}, bf16[2048,256]{0,1:T(8,128)(2,1)}, u32[]{:S(2)}) copy-start(bf16[2048,256]{0,1:T(8,128)(2,1)} %copy.16) | copy-start | bytes 3145732
Sparse Core Ops, SparseCore 0:
  9.5 131.2 all-gather.2
  143.0 186.2 all-gather.4
  333.8 89.2 reduce-scatter.1
where the time goes:
time: 430 us
  waiting for transfers between devices  366 us (85%)
  starting transfers between devices  19.9 us (5%)
  matrix products  14.8 us (3%)
  between operations  13.4 us (3%)
  other arithmetic  8.11 us (2%)
  local copies, waits for them, and re-layouts  7.23 us (2%)
    all_gather x1, waiting for transfers between devices, per_device(): lax.all_gather(w_qkv, 'tile', axis=1, tiled=True)  130 us
    all_gather x1, waiting for transfers between devices, per_device(): lax.all_gather(w_out, 'tile', axis=1, tiled=True)  96.7 us
    reduce_scatter x1, waiting for transfers between devices, per_device(): lax.psum_scatter(terms.astype(jnp.bfloat16), 'tensor', scatter_dimension=...  90.2 us
    ppermute x5, waiting for transfers between devices, from_behind(): return lax.ppermute(shard, axis, pairs)  48.2 us
    ppermute x5, starting transfers between devices, from_behind(): return lax.ppermute(shard, axis, pairs)  19.8 us
  transfers between devices with their start and end apart: 8, of which 8 were waited for; matrix products, arithmetic and copies ran while one was open for 6% of the time, Pallas kernels for 0%

commit v1 on v0

v1 whole, which is shorter than its diff:
```python
import functools

import jax
import jax.numpy as jnp
from jax import lax
from jax.experimental import pallas as pl
from jax.experimental.pallas import tpu as pltpu
from jax.sharding import PartitionSpec as P

MESH = pl.DeviceIdType.MESH
F32 = jnp.float32
BF16 = jnp.bfloat16
NZ = 16
SCALE = 128.0 ** -0.5


def kernel(win, tok_in, w_in, wo_in, out, tok, w, acc, kv, qs, mask, os, ts, attf, att, pk, wo,
           s_tok, s_init, s_bp, s_bm, s_ap, s_am, s_x, s_t, s_h, s_xe, s_wa, s_wc, s_ac, s_ax, s_ay):
    ti = lax.axis_index("tile")
    te = lax.axis_index("tensor")
    z, xl, c = ti // 4, (ti // 2) % 2, ti % 2
    xh, y = te // 4, te % 4
    t, h = z // 4, z % 4

    def at(z_, xl_, c_, xh_, y_):
        return (z_ * 4 + xl_ * 2 + c_, xh_ * 4 + y_)

    mate = at(z, xl, 1 - c, xh, y)
    side = at(z, 1 - xl, c, xh, y)
    side_mate = at(z, 1 - xl, 1 - c, xh, y)
    z_next = at((z + 1) % NZ, xl, c, xh, y)
    z_prev = at((z + NZ - 1) % NZ, xl, c, xh, y)
    later = at((z + 4) % NZ, xl, c, xh, y)
    earlier = at((z + NZ - 4) % NZ, xl, c, xh, y)

    def rc(src, dst, sems, i, dev):
        return pltpu.make_async_remote_copy(
            src_ref=src, dst_ref=dst, send_sem=sems.at[0, i], recv_sem=sems.at[1, i],
            device_id=dev, device_id_type=MESH)

    own_tok = pltpu.make_async_copy(tok_in, tok.at[c], s_tok.at[0, 1])
    own_tok.start()
    kv[...] = jnp.zeros_like(kv)

    bar = pltpu.get_barrier_semaphore()

    def greet(dev):
        pl.semaphore_signal(bar, inc=1, device_id=dev, device_id_type=MESH)

    for dev in (mate, side_mate, z_next, z_prev, later, earlier):
        greet(dev)
    for dx in range(4):
        for dy in range(4):
            if dx or dy:
                greet(at(z, xl ^ (dx & 1), c, xh ^ (dx >> 1), (y + dy) % 4))

    rows = pl.ds(pl.multiple_of(xl * 128, 128), 128)
    r0 = pl.ds(pl.multiple_of(xl * 128 + c * 64, 64), 64)
    mine = pl.ds(pl.multiple_of(c * 128, 128), 128)
    theirs = pl.ds(pl.multiple_of((1 - c) * 128, 128), 128)
    for j in range(3):
        w[z, j, r0, :] = w_in[j, :, mine]
    own_rows = wo_in[pl.ds(pl.multiple_of(c * 128, 128), 128), :]
    other_rows = wo_in[pl.ds(pl.multiple_of((1 - c) * 128, 128), 128), :]
    pk[0] = jnp.concatenate([other_rows, other_rows], axis=1)
    pl.semaphore_wait(bar, 21)

    i_mate = rc(w_in.at[:, :, theirs], w.at[z, pl.ds(0, 3), r0, :], s_init, 0, mate)
    i_side = rc(w_in.at[0, :, mine], w.at[z, 0, r0, :], s_init, 1, side)
    i_diag = rc(w_in.at[0, :, theirs], w.at[z, 0, r0, :], s_init, 2, side_mate)
    i_out = rc(pk.at[0], pk.at[1], s_init, 3, mate)
    i_mate.start()
    i_out.start()
    i_side.start()
    i_diag.start()
    tok_x = rc(tok_in, tok.at[c], s_tok, 0, mate)
    tok_x.start()

    i_mate.wait_recv()
    i_out.wait_recv()
    from_mate = pk[1]
    lane = lax.broadcasted_iota(jnp.int32, (128, 128), 1)
    own2 = jnp.concatenate([own_rows, own_rows], axis=1).astype(F32)
    keep = jnp.where(c == 0, lane, 127 - lane) < 64
    w[z, 3, rows, :] = jnp.where(keep, own2, from_mate.astype(F32)).astype(BF16)

    def part_b(zo):
        return w.at[zo, pl.ds(1, 3), rows, :]

    def part_a(zo):
        return w.at[zo, 0]

    def part_x(zo):
        return w.at[zo, pl.ds(1, 2), rows, :]

    def send_b(zo, sems, i, dev):
        return rc(part_b(zo), part_b(zo), sems, i, dev)

    def send_a(zo, sems, i, dev):
        return rc(part_a(zo), part_a(zo), sems, i, dev)

    def send_x(zo, i):
        return rc(part_x(zo), part_x(zo), s_x, i, side)

    send_b(z, s_bp, 0, z_next).start()
    send_b(z, s_bm, 0, z_prev).start()
    send_x(z, 0).start()
    i_side.wait_recv()
    i_diag.wait_recv()
    send_a(z, s_ap, 0, z_next).start()
    send_a(z, s_am, 0, z_prev).start()

    rh, rw, rt = win[c, 1], win[c, 2], win[c, 0]
    qi = lax.broadcasted_iota(jnp.int32, (64, 384), 0)
    ki = lax.broadcasted_iota(jnp.int32, (64, 384), 1)
    grp = ki // 128
    krow = (ki % 128) // 8
    d_r = jnp.abs(krow - 4 - qi // 8)
    d_c = jnp.abs((grp - 1) * 8 + ki % 8 - qi % 8)
    grow = h * 8 + krow - 4
    near = (d_r <= rh) & (d_c <= rw) & (grow >= 0) & (grow < 32)
    for u in range(4):
        gcol = xl * 4 + u + grp - 1
        mask[u] = jnp.where(near & (gcol >= 0) & (gcol < 8), F32(1.0), F32(0.0))

    def allow(a, f):
        df = 2 + a - f
        ok = jnp.where(rt >= df, F32(1.0), F32(0.0))
        if f < 2:
            ok = jnp.where(t > 0, ok, F32(0.0))
        return ok

    own_tok.wait()
    tok_x.wait_recv()

    def project(zo):
        cols = pl.ds(pl.multiple_of(zo * 256, 256), 256)
        lhs = tok[:, :, cols].reshape(512, 256)
        rhs = jnp.concatenate([w[zo, 0], w[zo, 1], w[zo, 2]], axis=1)
        return jnp.dot(lhs, rhs, preferred_element_type=F32)

    send_x(z, 0).wait_recv()
    acc[...] = project(z)

    def fwd(s, _):
        zp = (z + NZ - s) % NZ
        zm = (z + s) % NZ

        @pl.when(s < 8)
        def _():
            send_b(zp, s_bp, s - 1, z_next).wait_recv()

            @pl.when(s < 7)
            def _():
                send_b(zp, s_bp, s, z_next).start()
            send_x(zp, s).start()

        send_b(zm, s_bm, s - 1, z_prev).wait_recv()

        @pl.when(s < 8)
        def _():
            send_b(zm, s_bm, s, z_prev).start()
        send_x(zm, 7 + s).start()

        send_a(zp, s_ap, s - 1, z_next).wait_recv()

        @pl.when(s < 8)
        def _():
            send_a(zp, s_ap, s, z_next).start()
            send_a(zm, s_am, s - 1, z_prev).wait_recv()

            @pl.when(s < 7)
            def _():
                send_a(zm, s_am, s, z_prev).start()

        @pl.when(s > 1)
        def _():
            zq = (z + NZ - s + 1) % NZ
            send_x(zq, s - 1).wait_recv()
            acc[...] += project(zq)
            zr = (z + s - 1) % NZ
            send_x(zr, 6 + s).wait_recv()
            acc[...] += project(zr)
        return 0

    lax.fori_loop(1, 9, fwd, 0)
    z8 = (z + 8) % NZ
    send_x(z8, 15).wait_recv()
    acc[...] += project(z8)

    def unit(p):
        return p * lax.rsqrt(jnp.mean(p * p, axis=-1, keepdims=True) + 1e-06)

    for tw in range(2):
        for a in range(2):
            at_rows = pl.ds(tw * 256 + a * 128, 128)
            both = jnp.concatenate([unit(acc[at_rows, 128:256]), acc[at_rows, 256:384]], axis=1)
            both = both.reshape(8, 2, 8, 256)
            for g in range(2):
                kv[2 + a, 1 + tw * 2 + g, 32:96, :] = both[:, g].reshape(64, 256).astype(BF16)

    edge_out = 4 - 3 * xl
    edge_in = 5 * xl
    OWN, TOP, BOT = pl.ds(32, 64), pl.ds(0, 32), pl.ds(96, 32)
    MIDG = pl.ds(1, 4)

    def t_halo(f):
        return rc(kv.at[2 + f, MIDG, OWN, :], kv.at[f, MIDG, OWN, :], s_t, f, later)

    def h_down(p):
        fr = pl.ds(2 * p, 2)
        return rc(kv.at[fr, MIDG, pl.ds(64, 32), :], kv.at[fr, MIDG, TOP, :], s_h, p, z_next)

    def h_up(p):
        fr = pl.ds(2 * p, 2)
        return rc(kv.at[fr, MIDG, pl.ds(32, 32), :], kv.at[fr, MIDG, BOT, :], s_h, 2 + p, z_prev)

    def x_edge(p, part):
        fr = pl.ds(2 * p, 2)
        rws = (OWN, TOP, BOT)[part]
        return rc(kv.at[fr, edge_out, rws, :], kv.at[fr, edge_in, rws, :], s_xe, p * 3 + part, side)

    has_prev, has_later = t > 0, t < 3
    has_up, has_down = h > 0, h < 3

    @pl.when(has_down)
    def _():
        h_down(1).start()

    @pl.when(has_up)
    def _():
        h_up(1).start()

    @pl.when(has_later)
    def _():
        t_halo(1).start()
        t_halo(0).start()

    x_edge(1, 0).start()

    def wa(dx, dy):
        xh2, y2 = xh ^ (dx >> 1), (y + dy) % 4
        j2 = xh2 * 4 + y2
        src = w.at[pl.ds(2 * j2, 2), 3, rows, :]
        return rc(src, wo.at[c, xh * 4 + y, xl], s_wa, dx * 4 + dy, at(z, xl ^ (dx & 1), c, xh2, y2))

    for dx in range(4):
        for dy in range(4):
            if dx or dy:
                wa(dx, dy).start()
    own_wo = pltpu.make_async_copy(w.at[pl.ds(2 * te, 2), 3, rows, :], wo.at[c, te, xl], s_wa.at[0, 0])
    own_wo.start()

    for tw in range(2):
        for a in range(2):
            q = unit(acc[pl.ds(tw * 256 + a * 128, 128), 0:128]).reshape(8, 2, 8, 128)
            for g in range(2):
                qs[tw * 2 + g, a] = q[:, g].reshape(64, 128).astype(BF16)

    @pl.when(has_up)
    def _():
        h_down(1).wait_recv()
        x_edge(1, 1).start()

    @pl.when(has_down)
    def _():
        h_up(1).wait_recv()
        x_edge(1, 2).start()

    x_edge(1, 0).wait_recv()

    @pl.when(has_up)
    def _():
        x_edge(1, 1).wait_recv()

    @pl.when(has_down)
    def _():
        x_edge(1, 2).wait_recv()

    def attend(u, a, f):
        keys = kv[f, u:u + 3, :, 0:128].reshape(384, 128)
        vals = kv[f, u:u + 3, :, 128:256].reshape(384, 128)
        s = lax.dot_general(qs[u, a], keys, (((1,), (1,)), ((), ())), preferred_element_type=F32)
        wt = jnp.exp(s * SCALE) * (mask[u] * allow(a, f))
        part = wt[:, 0:128] + wt[:, 128:256] + wt[:, 256:384]
        return jnp.dot(wt.astype(BF16), vals, preferred_element_type=F32), part

    for u in range(4):
        o, p = attend(u, 0, 2)
        os[u, 0] = o
        ts[u, 0] = p
        o2, p2 = attend(u, 1, 2)
        o3, p3 = attend(u, 1, 3)
        os[u, 1] = o2 + o3
        ts[u, 1] = p2 + p3

    @pl.when(has_prev)
    def _():
        t_halo(1).wait_recv()
        t_halo(0).wait_recv()

        @pl.when(has_down)
        def _():
            h_down(0).start()

        @pl.when(has_up)
        def _():
            h_up(0).start()
        x_edge(0, 0).start()

        @pl.when(has_up)
        def _():
            h_down(0).wait_recv()
            x_edge(0, 1).start()

        @pl.when(has_down)
        def _():
            h_up(0).wait_recv()
            x_edge(0, 2).start()
        x_edge(0, 0).wait_recv()

        @pl.when(has_up)
        def _():
            x_edge(0, 1).wait_recv()

        @pl.when(has_down)
        def _():
            x_edge(0, 2).wait_recv()

    for u in range(4):
        for a in range(2):
            o, p = attend(u, a, 1)
            if a == 0:
                o2, p2 = attend(u, 0, 0)
                o, p = o + o2, p + p2
            total = jnp.sum(ts[u, a] + p, axis=-1, keepdims=True)
            res = (os[u, a] + o) / total
            attf[u // 2, a, :, u % 2] = res.reshape(8, 8, 128)

    for tw in range(2):
        pk2 = attf[tw].reshape(256, 128).astype(BF16)
        ts_dst = att.at[8 + tw]
        ts_dst[0] = pk2

    a_mate = rc(att.at[9 - c, 0], att.at[te, c], s_ac, 0, mate)
    a_mate.start()
    att[te, c] = att[8 + c, 0]
    a_mate.wait_recv()

    def a_side(j, i, dev):
        return rc(att.at[j], att.at[j], s_ay, i, dev)

    te_x = (1 - xh) * 4 + y
    ax = rc(att.at[te], att.at[te], s_ax, 0, at(z, xl, c, 1 - xh, y))
    ax.start()
    for dy in (1, 3, 2):
        a_side(te, dy, at(z, xl, c, xh, (y + dy) % 4)).start()

    own_wo.wait()
    for dx in range(4):
        for dy in range(4):
            if dx or dy:
                rc(w.at[pl.ds(0, 2), 3, rows, :], wo.at[c, 0, 0], s_wa, dx * 4 + dy, mate).wait_recv()
    wo_x = rc(wo.at[c], wo.at[c], s_wc, 0, mate)
    wo_x.start()

    ax.wait_recv()
    for dy in (1, 3, 2):
        a_side(te_x, 4 + dy, at(z, xl, c, xh, (y + dy) % 4)).start()
    wo_x.wait_recv()

    def term(j):
        lhs = jnp.concatenate([att[j, 0], att[j, 1]], axis=1)
        rhs = jnp.concatenate([
            jnp.concatenate([wo[p, j, 0, 0], wo[p, j, 1, 0], wo[p, j, 0, 1], wo[p, j, 1, 1]], axis=1)
            for p in range(2)], axis=0)
        return jnp.dot(lhs, rhs, preferred_element_type=F32)

    fin = acc.at[pl.ds(0, 256), :]
    fin2 = acc.at[pl.ds(256, 256), :]

    def add(j, first=False):
        r = term(j)
        if first:
            fin[...] = r[:, 0:384]
            fin2[:, 0:128] = r[:, 384:512]
        else:
            fin[...] += r[:, 0:384]
            fin2[:, 0:128] += r[:, 384:512]

    add(te, True)
    add(te_x)
    for k in range(2):
        for dy in (1, 3, 2):
            a_side(te, 4 * k + dy, mate).wait_recv()
            xs = xh if k == 0 else 1 - xh
            add(xs * 4 + (y + 4 - dy) % 4)
    out[:, 0:384] = fin[...].astype(BF16)
    out[:, 384:512] = fin2[:, 0:128].astype(BF16)

    for d in (i_mate, i_side, i_diag, i_out, tok_x, a_mate, ax, wo_x):
        d.wait_send()

    def drain(s, _):
        send_x(z, s).wait_send()

        @pl.when(s < 8)
        def _():
            send_b(z, s_bm, s, z_prev).wait_send()
            send_a(z, s_ap, s, z_next).wait_send()

        @pl.when(s < 7)
        def _():
            send_b(z, s_bp, s, z_next).wait_send()
            send_a(z, s_am, s, z_prev).wait_send()
        return 0

    lax.fori_loop(0, 16, drain, 0)
    for dx in range(4):
        for dy in range(4):
            if dx or dy:
                wa(dx, dy).wait_send()
    for k in range(2):
        for dy in (1, 3, 2):
            a_side(te, 4 * k + dy, mate).wait_send()
    x_edge(1, 0).wait_send()

    @pl.when(has_later)
    def _():
        t_halo(0).wait_send()
        t_halo(1).wait_send()

    @pl.when(has_prev)
    def _():
        x_edge(0, 0).wait_send()

    @pl.when(has_down)
    def _():
        h_down(1).wait_send()
        x_edge(1, 2).wait_send()

        @pl.when(has_prev)
        def _():
            h_down(0).wait_send()
            x_edge(0, 2).wait_send()

    @pl.when(has_up)
    def _():
        h_up(1).wait_send()
        x_edge(1, 1).wait_send()

        @pl.when(has_prev)
        def _():
            h_up(0).wait_send()
            x_edge(0, 1).wait_send()


def per_device(tokens, w_qkv, w_out, window_ext):
    vm = pl.BlockSpec(memory_space=pltpu.VMEM)
    dma = lambda n: pltpu.SemaphoreType.DMA((2, n))
    return pl.pallas_call(
        kernel,
        out_shape=jax.ShapeDtypeStruct((256, 512), BF16),
        in_specs=[pl.BlockSpec(memory_space=pltpu.SMEM), pl.BlockSpec(memory_space=pl.ANY), vm, vm],
        out_specs=vm,
        scratch_shapes=[
            pltpu.VMEM((2, 256, 4096), BF16),
            pltpu.VMEM((16, 4, 256, 128), BF16),
            pltpu.VMEM((512, 384), F32),
            pltpu.VMEM((4, 6, 128, 256), BF16),
            pltpu.VMEM((4, 2, 64, 128), BF16),
            pltpu.VMEM((4, 64, 384), F32),
            pltpu.VMEM((4, 2, 64, 128), F32),
            pltpu.VMEM((4, 2, 64, 128), F32),
            pltpu.VMEM((2, 2, 8, 2, 8, 128), F32),
            pltpu.VMEM((10, 2, 256, 128), BF16),
            pltpu.VMEM((2, 128, 128), BF16),
            pltpu.VMEM((2, 8, 2, 2, 128, 128), BF16),
            dma(2), dma(4), dma(8), dma(8), dma(8), dma(8), dma(16), dma(2), dma(4), dma(6),
            dma(16), dma(1), dma(1), dma(1), dma(8),
        ],
        compiler_params=pltpu.CompilerParams(
            collective_id=0, has_side_effects=True, vmem_limit_bytes=56 * 2 ** 20),
        name="tile_attention",
    )(window_ext, tokens, w_qkv, w_out)


def solution(mesh):
    in_specs = (P("tile", None), P(None, "tile", "tensor"), P("tensor", "tile"), P("tensor", None))
    return jax.shard_map(
        per_device, mesh=mesh, in_specs=in_specs, out_specs=P("tile", "tensor"), check_vma=False)
```

time: 430 us -> 104 us (0.24)
  the two profiles are of different devices: /device:TPU:32 before, /device:TPU:417 now
where the time goes in v1:
time: 104 us; the launch traced here: 103 us
  Pallas kernels  100 us (96%)
  local copies, waits for them, and re-layouts  3.16 us (3%)
    pallas_call x1, Pallas kernels, per_device(): pl.pallas_call(kernel, out_shape=jax.ShapeDtypeStruct((256, 512), BF16),...  100 us
    unnamed x2, local copies, waits for them, and re-layouts  3.16 us

profile of v1, /device:TPU:417, one launch (start us, length us, event | category | flops | bytes accessed | tf_op | source)
XLA Modules:
  0.0 103.5 jit_solution(6587831534853413149)
XLA Ops:
  0.0 1.5 %copy.5.wo_in = bf16[256,64]{1,0:T(8,128)(2,1)} copy(bf16[256,64]{0,1:T(8,128)(2,1)} %param.6) | data formatting | bytes 65536 | tf_op args[2]
  1.5 100.3 %tile_attention.1 = bf16[256,512]{1,0:T(8,128)(2,1)} custom-call(s32[2,3]{1,0:T(2,128)} %win.1, bf16[256,4096]{1,0:T(8,128)(2,1)} %tok_in.1, bf16[3,64,256]{2,1,0:T(8,128)(2,1)} %w_in.1, bf16[256,64]{1,0:T(8,128)(2,1)} %copy.5.wo_in), custom_call_target="tpu_custom_call" | custom-call | tf_op jit(solution)/shard_map/tile_attention/pallas_call | solution.py:461
  101.8 1.7 %copy.7 = bf16[256,512]{1,0:T(8,128)(2,1)} copy(bf16[256,512]{1,0:T(8,128)(2,1)} %tile_attention.1) | data formatting | bytes 524288

commit v2 on v1

v2 whole, which is shorter than its diff:
```python
import functools

import jax
import jax.numpy as jnp
from jax import lax
from jax.experimental import pallas as pl
from jax.experimental.pallas import tpu as pltpu
from jax.sharding import PartitionSpec as P

MESH = pl.DeviceIdType.MESH
F32 = jnp.float32
BF16 = jnp.bfloat16
NZ = 16
SCALE = 128.0 ** -0.5


def kernel(win, tok_in, w_in, wo_in, out, tok, w, acc, kv, qs, mask, os, ts, attf, att, tmp, wo, fin,
           s_tok, s_init, s_zp, s_zm, s_x, s_t, s_h, s_xe, s_wa, s_wc, s_ag):
    ti = lax.axis_index("tile")
    te = lax.axis_index("tensor")
    z, xl, c = ti // 4, (ti // 2) % 2, ti % 2
    xh, y = te // 4, te % 4
    t, h = z // 4, z % 4

    def at(z_, xl_, c_, xh_, y_):
        return (z_ * 4 + xl_ * 2 + c_, xh_ * 4 + y_)

    zn, zv = (z + 1) % NZ, (z + NZ - 1) % NZ
    mate = at(z, xl, 1 - c, xh, y)
    side = at(z, 1 - xl, c, xh, y)
    side_mate = at(z, 1 - xl, 1 - c, xh, y)
    z_next = at(zn, xl, c, xh, y)
    z_prev = at(zv, xl, c, xh, y)
    side_next = at(zn, 1 - xl, c, xh, y)
    side_prev = at(zv, 1 - xl, c, xh, y)
    later = at((z + 4) % NZ, xl, c, xh, y)
    earlier = at((z + NZ - 4) % NZ, xl, c, xh, y)

    def rc(src, dst, sems, i, dev):
        return pltpu.make_async_remote_copy(
            src_ref=src, dst_ref=dst, send_sem=sems.at[0, i], recv_sem=sems.at[1, i],
            device_id=dev, device_id_type=MESH)

    def rc2(src, dst, si, ri, sems, dev):
        return pltpu.make_async_remote_copy(
            src_ref=src, dst_ref=dst, send_sem=sems.at[0, si], recv_sem=sems.at[1, ri],
            device_id=dev, device_id_type=MESH)

    rows = pl.ds(pl.multiple_of(xl * 128, 128), 128)
    others = pl.ds(pl.multiple_of((1 - xl) * 128, 128), 128)
    r0 = pl.ds(pl.multiple_of(xl * 128 + c * 64, 64), 64)
    mine = pl.ds(pl.multiple_of(c * 128, 128), 128)
    theirs = pl.ds(pl.multiple_of((1 - c) * 128, 128), 128)

    own_w = pltpu.make_async_copy(w_in.at[:, :, mine], w.at[z, pl.ds(0, 3), r0, :], s_tok.at[0, 2])
    own_o = pltpu.make_async_copy(wo_in.at[:, mine], w.at[z, 3, r0, :], s_tok.at[0, 3])
    own_tok = pltpu.make_async_copy(tok_in, tok.at[c], s_tok.at[0, 1])
    for d in (own_w, own_o, own_tok):
        d.start()

    bar = pltpu.get_barrier_semaphore()

    def greet(dev):
        pl.semaphore_signal(bar, inc=1, device_id=dev, device_id_type=MESH)

    kv[...] = jnp.zeros_like(kv)
    for dev in (later, earlier, z_next, z_prev, side_next, side_prev, side_mate, mate):
        greet(dev)
    for dx in range(4):
        for dy in range(4):
            if dx or dy:
                greet(at(z, xl ^ (dx & 1), c, xh ^ (dx >> 1), (y + dy) % 4))
    for dx, dy in ((2, 0), (0, 1), (0, 2), (0, 3)):
        greet(at(z, xl, 1 - c, xh ^ (dx >> 1), (y + dy) % 4))
    pl.semaphore_wait(bar, 27)

    i_mate = rc(w_in.at[:, :, theirs], w.at[z, pl.ds(0, 3), r0, :], s_init, 0, mate)
    i_side = rc(w_in.at[0, :, mine], w.at[z, 0, r0, :], s_init, 1, side)
    i_diag = rc(w_in.at[0, :, theirs], w.at[z, 0, r0, :], s_init, 2, side_mate)
    i_out = rc(wo_in.at[:, theirs], w.at[z, 3, r0, :], s_init, 3, mate)
    i_mate.start()
    i_out.start()
    i_side.start()
    i_diag.start()
    tok_x = rc(tok_in, tok.at[c], s_tok, 0, mate)
    tok_x.start()

    def chunk(zo, ch):
        return w.at[zo, (1, 2, 0, 0, 3)[ch], others if ch == 3 else rows, :]

    def zp_copy(zo, ch, s):
        return rc(chunk(zo, ch), chunk(zo, ch), s_zp, ch * 8 + s, z_next)

    def zm_copy(zo, ch, s):
        return rc(chunk(zo, ch), chunk(zo, ch), s_zm, ch * 8 + s, z_prev)

    def x_copy(zo, m, i):
        return rc(chunk(zo, m), chunk(zo, m), s_x, m * 16 + i, side)

    own_w.wait()
    i_mate.wait_recv()
    for ch in range(2):
        zp_copy(z, ch, 0).start()
        zm_copy(z, ch, 0).start()
        x_copy(z, ch, 0).start()
    zp_copy(z, 2, 0).start()
    zm_copy(z, 2, 0).start()
    own_o.wait()
    i_out.wait_recv()
    i_side.wait_recv()
    i_diag.wait_recv()
    for ch in (3, 4):
        zp_copy(z, ch, 0).start()
        zm_copy(z, ch, 0).start()

    rh, rw, rt = win[c, 1], win[c, 2], win[c, 0]
    qi = lax.broadcasted_iota(jnp.int32, (64, 384), 0)
    ki = lax.broadcasted_iota(jnp.int32, (64, 384), 1)
    grp = ki // 128
    krow = (ki % 128) // 8
    d_r = jnp.abs(krow - 4 - qi // 8)
    d_c = jnp.abs((grp - 1) * 8 + ki % 8 - qi % 8)
    grow = h * 8 + krow - 4
    near = (d_r <= rh) & (d_c <= rw) & (grow >= 0) & (grow < 32)
    for u in range(4):
        gcol = xl * 4 + u + grp - 1
        mask[u] = jnp.where(near & (gcol >= 0) & (gcol < 8), F32(1.0), F32(0.0))

    def allow(a, f):
        df = 2 + a - f
        ok = jnp.where(rt >= df, F32(1.0), F32(0.0))
        if f < 2:
            ok = jnp.where(t > 0, ok, F32(0.0))
        return ok

    def project(zo):
        cols = pl.ds(pl.multiple_of(zo * 256, 256), 256)
        lhs = tok[:, :, cols].reshape(512, 256)
        rhs = jnp.concatenate([w[zo, 0], w[zo, 1], w[zo, 2]], axis=1)
        return jnp.dot(lhs, rhs, preferred_element_type=F32)

    def fwd(s, _):
        zp = (z + NZ - s) % NZ
        zm = (z + s) % NZ

        for ch in range(5):
            q_part = ch in (2, 3)
            last_p, last_m = (8, 7) if q_part else (7, 8)

            @pl.when(s <= last_p)
            def _():
                zp_copy(zp, ch, s - 1).wait_recv()

                @pl.when(s < last_p)
                def _():
                    zp_copy(zp, ch, s).start()
                if ch < 2:
                    x_copy(zp, ch, s).start()

            @pl.when(s <= last_m)
            def _():
                zm_copy(zm, ch, s - 1).wait_recv()

                @pl.when(s < last_m)
                def _():
                    zm_copy(zm, ch, s).start()
                if ch < 2:
                    x_copy(zm, ch, 7 + s).start()

        @pl.when(s == 1)
        def _():
            own_tok.wait()
            tok_x.wait_recv()
            x_copy(z, 0, 0).wait_recv()
            x_copy(z, 1, 0).wait_recv()
            acc[...] = project(z)

        @pl.when(s > 1)
        def _():
            zq = (z + NZ - s + 1) % NZ
            x_copy(zq, 0, s - 1).wait_recv()
            x_copy(zq, 1, s - 1).wait_recv()
            acc[...] += project(zq)
            zr = (z + s - 1) % NZ
            x_copy(zr, 0, 6 + s).wait_recv()
            x_copy(zr, 1, 6 + s).wait_recv()
            acc[...] += project(zr)
        return 0

    lax.fori_loop(1, 9, fwd, 0)
    z8 = (z + 8) % NZ
    x_copy(z8, 0, 15).wait_recv()
    x_copy(z8, 1, 15).wait_recv()
    acc[...] += project(z8)

    def unit(p):
        return p * lax.rsqrt(jnp.mean(p * p, axis=-1, keepdims=True) + 1e-06)

    for tw in range(2):
        for a in range(2):
            at_rows = pl.ds(tw * 256 + a * 128, 128)
            both = jnp.concatenate([unit(acc[at_rows, 128:256]), acc[at_rows, 256:384]], axis=1)
            both = both.reshape(8, 2, 8, 256)
            for g in range(2):
                kv[2 + a, 1 + tw * 2 + g, 32:96, :] = both[:, g].reshape(64, 256).astype(BF16)

    edge_out = 4 - 3 * xl
    edge_in = 5 * xl
    OWN, TOP, BOT = pl.ds(32, 64), pl.ds(0, 32), pl.ds(96, 32)
    UP, DOWN = pl.ds(32, 32), pl.ds(64, 32)
    MIDG = pl.ds(1, 4)
    FRAMES = (pl.ds(2, 2), pl.ds(1, 1), pl.ds(0, 1))

    def t_halo(f):
        return rc(kv.at[2 + f, MIDG, OWN, :], kv.at[f, MIDG, OWN, :], s_t, f, later)

    def h_down(i):
        return rc(kv.at[FRAMES[i], MIDG, DOWN, :], kv.at[FRAMES[i], MIDG, TOP, :], s_h, i, z_next)

    def h_up(i):
        return rc(kv.at[FRAMES[i], MIDG, UP, :], kv.at[FRAMES[i], MIDG, BOT, :], s_h, 3 + i, z_prev)

    def x_own(i):
        return rc(kv.at[FRAMES[i], edge_out, OWN, :], kv.at[FRAMES[i], edge_in, OWN, :], s_xe, i, side)

    def x_down(i):
        return rc(kv.at[FRAMES[i], edge_out, DOWN, :], kv.at[FRAMES[i], edge_in, TOP, :], s_xe, 3 + i, side_next)

    def x_up(i):
        return rc(kv.at[FRAMES[i], edge_out, UP, :], kv.at[FRAMES[i], edge_in, BOT, :], s_xe, 6 + i, side_prev)

    has_prev, has_later = t > 0, t < 3
    has_up, has_down = h > 0, h < 3

    def halo_start(i):
        @pl.when(has_down)
        def _():
            h_down(i).start()
            x_down(i).start()

        @pl.when(has_up)
        def _():
            h_up(i).start()
            x_up(i).start()
        x_own(i).start()

    def halo_wait(i):
        x_own(i).wait_recv()

        @pl.when(has_up)
        def _():
            h_down(i).wait_recv()
            x_down(i).wait_recv()

        @pl.when(has_down)
        def _():
            h_up(i).wait_recv()
            x_up(i).wait_recv()

    def halo_sent(i):
        x_own(i).wait_send()

        @pl.when(has_down)
        def _():
            h_down(i).wait_send()
            x_down(i).wait_send()

        @pl.when(has_up)
        def _():
            h_up(i).wait_send()
            x_up(i).wait_send()

    @pl.when(has_later)
    def _():
        t_halo(1).start()
    halo_start(0)

    def wa(dx, dy):
        xh2, y2 = xh ^ (dx >> 1), (y + dy) % 4
        j2 = xh2 * 4 + y2
        src = w.at[pl.ds(2 * j2, 2), 3, rows, :]
        return rc(src, wo.at[c, xh * 4 + y, xl], s_wa, dx * 4 + dy, at(z, xl ^ (dx & 1), c, xh2, y2))

    for dx in range(4):
        for dy in range(4):
            if dx or dy:
                wa(dx, dy).start()
    own_wo = pltpu.make_async_copy(w.at[pl.ds(2 * te, 2), 3, rows, :], wo.at[c, te, xl], s_wa.at[0, 0])
    own_wo.start()

    for tw in range(2):
        for a in range(2):
            q = unit(acc[pl.ds(tw * 256 + a * 128, 128), 0:128]).reshape(8, 2, 8, 128)
            for g in range(2):
                qs[tw * 2 + g, a] = q[:, g].reshape(64, 128).astype(BF16)

    def attend(u, a, f):
        keys = kv[f, u:u + 3, :, 0:128].reshape(384, 128)
        vals = kv[f, u:u + 3, :, 128:256].reshape(384, 128)
        s = lax.dot_general(qs[u, a], keys, (((1,), (1,)), ((), ())), preferred_element_type=F32)
        wt = jnp.exp(s * SCALE) * (mask[u] * allow(a, f))
        part = wt[:, 0:128] + wt[:, 128:256] + wt[:, 256:384]
        return jnp.dot(wt.astype(BF16), vals, preferred_element_type=F32), part

    halo_wait(0)
    for u in range(4):
        o, p = attend(u, 0, 2)
        os[u, 0] = o
        ts[u, 0] = p
        o2, p2 = attend(u, 1, 2)
        o3, p3 = attend(u, 1, 3)
        os[u, 1] = o2 + o3
        ts[u, 1] = p2 + p3

    @pl.when(has_later)
    def _():
        t_halo(1).wait_send()
        t_halo(0).start()

    te_x = (1 - xh) * 4 + y

    def slot(a, k, dy, p):
        return ((a * 2 + k) * 4 + dy) * 2 + p

    def a_out(a, k, dy, own):
        src = att.at[te, c, a] if own else tmp.at[1 - c, a]
        dev = at(z, xl, c if own else 1 - c, 1 - xh if k else xh, (y + dy) % 4)
        return rc2(src, att.at[te, c, a], slot(a, k, dy, 0 if own else 1), slot(a, k, dy, c), s_ag, dev)

    def a_on(a, dy, p):
        return rc(att.at[te_x, p, a], att.at[te_x, p, a], s_ag, slot(a, 1, dy, p), at(z, xl, c, xh, (y + dy) % 4))

    def a_in(a, k, dy, p):
        return rc(att.at[te, p, a], att.at[te, p, a], s_ag, slot(a, k, dy, p), mate)

    def finish(a, f):
        for u in range(4):
            o, p = attend(u, a, f)
            total = jnp.sum(ts[u, a] + p, axis=-1, keepdims=True)
            res = (os[u, a] + o) / total
            attf[u // 2, :, u % 2] = res.reshape(8, 8, 128)
        for tw in range(2):
            tmp[tw, a] = attf[tw].reshape(128, 128).astype(BF16)
        att[te, c, a] = tmp[c, a]
        a_out(a, 1, 0, True).start()
        a_out(a, 1, 0, False).start()
        a_out(a, 0, 0, False).start()
        for dy in (1, 3, 2):
            a_out(a, 0, dy, True).start()
            a_out(a, 0, dy, False).start()

    def spread_on(a):
        for p in range(2):
            a_in(a, 1, 0, p).wait_recv()
            for dy in (1, 3, 2):
                a_on(a, dy, p).start()

    def term(j, a):
        lhs = jnp.concatenate([att[j, 0, a], att[j, 1, a]], axis=1)
        rhs = jnp.concatenate([
            jnp.concatenate([wo[0, j, x, k], wo[1, j, x, k]], axis=1)
            for k in range(2) for x in range(2)], axis=0)
        return lax.dot_general(lhs, rhs, (((1,), (1,)), ((), ())), preferred_element_type=F32)

    def mix(a):
        tot = fin.at[a]
        rc2(att.at[te, 0, a], att.at[te, 0, a], 0, slot(a, 0, 0, 1 - c), s_ag, mate).wait_recv()
        tot[...] = term(te, a)
        tot[...] += term(te_x, a)
        for k in range(2):
            for dy in (1, 3, 2):
                a_in(a, k, dy, 0).wait_recv()
                a_in(a, k, dy, 1).wait_recv()
                xs = xh if k == 0 else 1 - xh
                tot[...] += term(xs * 4 + (y + 4 - dy) % 4, a)
        out[a * 128:(a + 1) * 128, :] = tot[...].astype(BF16)

    @pl.when(has_prev)
    def _():
        t_halo(1).wait_recv()
        halo_start(1)

    own_wo.wait()
    for dx in range(4):
        for dy in range(4):
            if dx or dy:
                wa(dx, dy).wait_recv()
    wo_x = rc(wo.at[c], wo.at[c], s_wc, 0, mate)
    wo_x.start()

    @pl.when(has_prev)
    def _():
        halo_wait(1)
    finish(1, 1)

    for u in range(4):
        o, p = attend(u, 0, 1)
        os[u, 0] += o
        ts[u, 0] += p
    @pl.when(has_prev)
    def _():
        t_halo(0).wait_recv()
        halo_start(2)
    spread_on(1)

    @pl.when(has_prev)
    def _():
        halo_wait(2)
    finish(0, 0)
    spread_on(0)
    wo_x.wait_recv()
    mix(1)
    mix(0)

    for d in (i_mate, i_side, i_diag, i_out, tok_x, wo_x):
        d.wait_send()

    def drain(s, _):
        for m in range(2):
            x_copy(z, m, s).wait_send()

        @pl.when(s < 8)
        def _():
            for ch in range(5):
                (zp_copy if ch in (2, 3) else zm_copy)(z, ch, s).wait_send()

        @pl.when(s < 7)
        def _():
            for ch in range(5):
                (zm_copy if ch in (2, 3) else zp_copy)(z, ch, s).wait_send()
        return 0

    lax.fori_loop(0, 16, drain, 0)
    for dx in range(4):
        for dy in range(4):
            if dx or dy:
                wa(dx, dy).wait_send()
    for a in range(2):
        a_out(a, 1, 0, True).wait_send()
        a_out(a, 1, 0, False).wait_send()
        a_out(a, 0, 0, False).wait_send()
        for dy in (1, 3, 2):
            a_out(a, 0, dy, True).wait_send()
            a_out(a, 0, dy, False).wait_send()
            a_on(a, dy, 0).wait_send()
            a_on(a, dy, 1).wait_send()
    halo_sent(0)

    @pl.when(has_later)
    def _():
        t_halo(0).wait_send()

    @pl.when(has_prev)
    def _():
        halo_sent(1)
        halo_sent(2)


def per_device(tokens, w_qkv, w_out, window_ext):
    vm = pl.BlockSpec(memory_space=pltpu.VMEM)
    hbm = pl.BlockSpec(memory_space=pl.ANY)
    dma = lambda n: pltpu.SemaphoreType.DMA((2, n))
    return pl.pallas_call(
        kernel,
        out_shape=jax.ShapeDtypeStruct((256, 512), BF16),
        in_specs=[pl.BlockSpec(memory_space=pltpu.SMEM), hbm, hbm, hbm],
        out_specs=vm,
        scratch_shapes=[
            pltpu.VMEM((2, 256, 4096), BF16),
            pltpu.VMEM((16, 4, 256, 128), BF16),
            pltpu.VMEM((512, 384), F32),
            pltpu.VMEM((4, 6, 128, 256), BF16),
            pltpu.VMEM((4, 2, 64, 128), BF16),
            pltpu.VMEM((4, 64, 384), F32),
            pltpu.VMEM((4, 2, 64, 128), F32),
            pltpu.VMEM((4, 2, 64, 128), F32),
            pltpu.VMEM((2, 8, 2, 8, 128), F32),
            pltpu.VMEM((8, 2, 2, 128, 128), BF16),
            pltpu.VMEM((2, 2, 128, 128), BF16),
            pltpu.VMEM((2, 8, 2, 2, 128, 128), BF16),
            pltpu.VMEM((2, 128, 512), F32),
            dma(4), dma(4), dma(40), dma(40), dma(32), dma(2), dma(6), dma(9),
            dma(16), dma(1), dma(32),
        ],
        compiler_params=pltpu.CompilerParams(
            collective_id=0, has_side_effects=True, vmem_limit_bytes=56 * 2 ** 20),
        name="tile_attention",
    )(window_ext, tokens, w_qkv, w_out.T)


def solution(mesh):
    in_specs = (P("tile", None), P(None, "tile", "tensor"), P("tensor", "tile"), P("tensor", None))
    return jax.shard_map(
        per_device, mesh=mesh, in_specs=in_specs, out_specs=P("tile", "tensor"), check_vma=False)
```

time: 104 us -> 96.7 us (0.930)
  the two profiles are of different devices: /device:TPU:417 before, /device:TPU:160 now
where the time goes in v2:
time: 96.7 us; the launch traced here: 96.5 us
  Pallas kernels  94.8 us (98%)
  local copies, waits for them, and re-layouts  1.67 us (2%)
    pallas_call x1, Pallas kernels, per_device(): pl.pallas_call(kernel, out_shape=jax.ShapeDtypeStruct((256, 512), BF16),...  94.8 us

profile of v2, /device:TPU:160, one launch (start us, length us, event | category | flops | bytes accessed | tf_op | source)
XLA Modules:
  0.0 96.5 jit_solution(6531674606244162532)
XLA Ops:
  0.0 94.8 %tile_attention.1 = bf16[256,512]{1,0:T(8,128)(2,1)} custom-call(s32[2,3]{1,0:T(2,128)} %win.1, bf16[256,4096]{1,0:T(8,128)(2,1)} %tok_in.1, bf16[3,64,256]{2,1,0:T(8,128)(2,1)} %w_in.1, bf16[64,256]{1,0:T(8,128)(2,1)} %bitcast.1), custom_call_target="tpu_custom_call" | custom-call | tf_op jit(solution)/shard_map/tile_attention/pallas_call | solution.py:463
  94.8 1.7 %copy.6 = bf16[256,512]{1,0:T(8,128)(2,1)} copy(bf16[256,512]{1,0:T(8,128)(2,1)} %tile_attention.1) | data formatting | bytes 524288

commit v3 on v2

--- a/solution.py
+++ b/solution.py
@@ -11,11 +11,12 @@
 F32 = jnp.float32
 BF16 = jnp.bfloat16
 NZ = 16
+ROUTE = ((1, 2), (1, 1), (1, 3), (1, 0), (0, 2), (0, 1), (0, 3), (0, 0))
 SCALE = 128.0 ** -0.5
 
 
-def kernel(win, tok_in, w_in, wo_in, out, tok, w, acc, kv, qs, mask, os, ts, attf, att, tmp, wo, fin,
-           s_tok, s_init, s_zp, s_zm, s_x, s_t, s_h, s_xe, s_wa, s_wc, s_ag):
+def kernel(win, tok_in, w_in, wo_in, out, tok, w, acc, kv, qs, mask, os, ts, attf, att, tmp, wo, fin, relay,
+           s_tok, s_init, s_zp, s_zm, s_x, s_t, s_h, s_xe, s_wa, s_wc, s_ag, s_far):
     ti = lax.axis_index("tile")
     te = lax.axis_index("tensor")
     z, xl, c = ti // 4, (ti // 2) % 2, ti % 2
@@ -35,6 +36,8 @@
     side_prev = at(zv, 1 - xl, c, xh, y)
     later = at((z + 4) % NZ, xl, c, xh, y)
     earlier = at((z + NZ - 4) % NZ, xl, c, xh, y)
+    six_up = at((z + 6) % NZ, xl, c, xh, y)
+    six_down = at((z + NZ - 6) % NZ, xl, c, xh, y)
 
     def rc(src, dst, sems, i, dev):
         return pltpu.make_async_remote_copy(
@@ -64,15 +67,15 @@
         pl.semaphore_signal(bar, inc=1, device_id=dev, device_id_type=MESH)
 
     kv[...] = jnp.zeros_like(kv)
-    for dev in (later, earlier, z_next, z_prev, side_next, side_prev, side_mate, mate):
+    for dev in (six_up, six_down, later, earlier, z_next, z_prev, side_next, side_prev, side_mate, mate):
         greet(dev)
     for dx in range(4):
         for dy in range(4):
             if dx or dy:
                 greet(at(z, xl ^ (dx & 1), c, xh ^ (dx >> 1), (y + dy) % 4))
-    for dx, dy in ((2, 0), (0, 1), (0, 2), (0, 3)):
+    for dx, dy in ((2, 0), (0, 1), (0, 2), (0, 3), (2, 1), (2, 2), (2, 3)):
         greet(at(z, xl, 1 - c, xh ^ (dx >> 1), (y + dy) % 4))
-    pl.semaphore_wait(bar, 27)
+    pl.semaphore_wait(bar, 32)
 
     i_mate = rc(w_in.at[:, :, theirs], w.at[z, pl.ds(0, 3), r0, :], s_init, 0, mate)
     i_side = rc(w_in.at[0, :, mine], w.at[z, 0, r0, :], s_init, 1, side)
@@ -139,33 +142,43 @@
         rhs = jnp.concatenate([w[zo, 0], w[zo, 1], w[zo, 2]], axis=1)
         return jnp.dot(lhs, rhs, preferred_element_type=F32)
 
+    def take(s, ch):
+        zp, zm = (z + NZ - s) % NZ, (z + s) % NZ
+        last_p, last_m = (8, 7) if ch in (2, 3) else (7, 8)
+
+        @pl.when(s <= last_p)
+        def _():
+            zp_copy(zp, ch, s - 1).wait_recv()
+
+            @pl.when(s < last_p)
+            def _():
+                zp_copy(zp, ch, s).start()
+            if ch < 2:
+                x_copy(zp, ch, s).start()
+
+        @pl.when(s <= last_m)
+        def _():
+            zm_copy(zm, ch, s - 1).wait_recv()
+
+            @pl.when(s < last_m)
+            def _():
+                zm_copy(zm, ch, s).start()
+            if ch < 2:
+                x_copy(zm, ch, 7 + s).start()
+
+    def both_sides(s):
+        zq = (z + NZ - s) % NZ
+        x_copy(zq, 0, s).wait_recv()
+        x_copy(zq, 1, s).wait_recv()
+        acc[...] += project(zq)
+        zr = (z + s) % NZ
+        x_copy(zr, 0, 7 + s).wait_recv()
+        x_copy(zr, 1, 7 + s).wait_recv()
+        acc[...] += project(zr)
+
     def fwd(s, _):
-        zp = (z + NZ - s) % NZ
-        zm = (z + s) % NZ
-
         for ch in range(5):
-            q_part = ch in (2, 3)
-            last_p, last_m = (8, 7) if q_part else (7, 8)
-
-            @pl.when(s <= last_p)
-            def _():
-                zp_copy(zp, ch, s - 1).wait_recv()
-
-                @pl.when(s < last_p)
-                def _():
-                    zp_copy(zp, ch, s).start()
-                if ch < 2:
-                    x_copy(zp, ch, s).start()
-
-            @pl.when(s <= last_m)
-            def _():
-                zm_copy(zm, ch, s - 1).wait_recv()
-
-                @pl.when(s < last_m)
-                def _():
-                    zm_copy(zm, ch, s).start()
-                if ch < 2:
-                    x_copy(zm, ch, 7 + s).start()
+            take(s, ch)
 
         @pl.when(s == 1)
         def _():
@@ -177,21 +190,18 @@
 
         @pl.when(s > 1)
         def _():
-            zq = (z + NZ - s + 1) % NZ
-            x_copy(zq, 0, s - 1).wait_recv()
-            x_copy(zq, 1, s - 1).wait_recv()
-            acc[...] += project(zq)
-            zr = (z + s - 1) % NZ
-            x_copy(zr, 0, 6 + s).wait_recv()
-            x_copy(zr, 1, 6 + s).wait_recv()
-            acc[...] += project(zr)
+            both_sides(s - 1)
         return 0
 
-    lax.fori_loop(1, 9, fwd, 0)
+    lax.fori_loop(1, 8, fwd, 0)
+    take(8, 0)
+    take(8, 1)
+    both_sides(7)
     z8 = (z + 8) % NZ
     x_copy(z8, 0, 15).wait_recv()
     x_copy(z8, 1, 15).wait_recv()
-    acc[...] += project(z8)
+    lhs8 = tok[:, :, pl.ds(pl.multiple_of(z8 * 256, 256), 256)].reshape(512, 256)
+    acc[:, 128:384] += jnp.dot(lhs8, jnp.concatenate([w[z8, 1], w[z8, 2]], axis=1), preferred_element_type=F32)
 
     def unit(p):
         return p * lax.rsqrt(jnp.mean(p * p, axis=-1, keepdims=True) + 1e-06)
@@ -212,7 +222,12 @@
     FRAMES = (pl.ds(2, 2), pl.ds(1, 1), pl.ds(0, 1))
 
     def t_halo(f):
-        return rc(kv.at[2 + f, MIDG, OWN, :], kv.at[f, MIDG, OWN, :], s_t, f, later)
+        grp = MIDG if f else pl.ds(1, 3)
+        return rc(kv.at[2 + f, grp, OWN, :], kv.at[f, grp, OWN, :], s_t, f, later)
+
+    far_1 = rc(kv.at[2, 4, OWN, :], relay, s_far, 0, six_down)
+    far_2 = rc(relay, kv.at[0, 4, OWN, :], s_far, 1, six_down)
+    has_relay = (z + 6) % NZ < 12
 
     def h_down(i):
         return rc(kv.at[FRAMES[i], MIDG, DOWN, :], kv.at[FRAMES[i], MIDG, TOP, :], s_h, i, z_next)
@@ -272,8 +287,12 @@
 
     @pl.when(has_later)
     def _():
+        far_1.start()
         t_halo(1).start()
     halo_start(0)
+
+    for ch in (2, 3, 4):
+        take(8, ch)
 
     def wa(dx, dy):
         xh2, y2 = xh ^ (dx >> 1), (y + dy) % 4
@@ -288,6 +307,8 @@
     own_wo = pltpu.make_async_copy(w.at[pl.ds(2 * te, 2), 3, rows, :], wo.at[c, te, xl], s_wa.at[0, 0])
     own_wo.start()
 
+    acc[:, 0:128] += jnp.dot(
+        tok[:, :, pl.ds(pl.multiple_of(z8 * 256, 256), 256)].reshape(512, 256), w[z8, 0], preferred_element_type=F32)
     for tw in range(2):
         for a in range(2):
             q = unit(acc[pl.ds(tw * 256 + a * 128, 128), 0:128]).reshape(8, 2, 8, 128)
@@ -314,7 +335,6 @@
 
     @pl.when(has_later)
     def _():
-        t_halo(1).wait_send()
         t_halo(0).start()
 
     te_x = (1 - xh) * 4 + y
@@ -326,9 +346,6 @@
         src = att.at[te, c, a] if own else tmp.at[1 - c, a]
         dev = at(z, xl, c if own else 1 - c, 1 - xh if k else xh, (y + dy) % 4)
         return rc2(src, att.at[te, c, a], slot(a, k, dy, 0 if own else 1), slot(a, k, dy, c), s_ag, dev)
-
-    def a_on(a, dy, p):
-        return rc(att.at[te_x, p, a], att.at[te_x, p, a], s_ag, slot(a, 1, dy, p), at(z, xl, c, xh, (y + dy) % 4))
 
     def a_in(a, k, dy, p):
         return rc(att.at[te, p, a], att.at[te, p, a], s_ag, slot(a, k, dy, p), mate)
@@ -342,18 +359,10 @@
         for tw in range(2):
             tmp[tw, a] = attf[tw].reshape(128, 128).astype(BF16)
         att[te, c, a] = tmp[c, a]
-        a_out(a, 1, 0, True).start()
-        a_out(a, 1, 0, False).start()
-        a_out(a, 0, 0, False).start()
-        for dy in (1, 3, 2):
-            a_out(a, 0, dy, True).start()
-            a_out(a, 0, dy, False).start()
-
-    def spread_on(a):
-        for p in range(2):
-            a_in(a, 1, 0, p).wait_recv()
-            for dy in (1, 3, 2):
-                a_on(a, dy, p).start()
+        for k, dy in ROUTE:
+            if k or dy:
+                a_out(a, k, dy, True).start()
+            a_out(a, k, dy, False).start()
 
     def term(j, a):
         lhs = jnp.concatenate([att[j, 0, a], att[j, 1, a]], axis=1)
@@ -364,15 +373,15 @@
 
     def mix(a):
         tot = fin.at[a]
-        rc2(att.at[te, 0, a], att.at[te, 0, a], 0, slot(a, 0, 0, 1 - c), s_ag, mate).wait_recv()
-        tot[...] = term(te, a)
-        tot[...] += term(te_x, a)
-        for k in range(2):
-            for dy in (1, 3, 2):
+        for k, dy in ROUTE[::-1]:
+            if k or dy:
                 a_in(a, k, dy, 0).wait_recv()
                 a_in(a, k, dy, 1).wait_recv()
-                xs = xh if k == 0 else 1 - xh
+                xs = 1 - xh if k else xh
                 tot[...] += term(xs * 4 + (y + 4 - dy) % 4, a)
+            else:
+                rc2(att.at[te, 0, a], att.at[te, 0, a], 0, slot(a, 0, 0, 1 - c), s_ag, mate).wait_recv()
+                tot[...] = term(te, a)
         out[a * 128:(a + 1) * 128, :] = tot[...].astype(BF16)
 
     @pl.when(has_prev)
@@ -380,6 +389,20 @@
         t_halo(1).wait_recv()
         halo_start(1)
 
+    @pl.when(has_relay)
+    def _():
+        far_1.wait_recv()
+        far_2.start()
+
+    @pl.when(has_prev)
+    def _():
+        halo_wait(1)
+    finish(1, 1)
+
+    for u in range(4):
+        o, p = attend(u, 0, 1)
+        os[u, 0] += o
+        ts[u, 0] += p
     own_wo.wait()
     for dx in range(4):
         for dy in range(4):
@@ -390,24 +413,14 @@
 
     @pl.when(has_prev)
     def _():
-        halo_wait(1)
-    finish(1, 1)
-
-    for u in range(4):
-        o, p = attend(u, 0, 1)
-        os[u, 0] += o
-        ts[u, 0] += p
-    @pl.when(has_prev)
-    def _():
         t_halo(0).wait_recv()
+        far_2.wait_recv()
         halo_start(2)
-    spread_on(1)
 
     @pl.when(has_prev)
     def _():
         halo_wait(2)
     finish(0, 0)
-    spread_on(0)
     wo_x.wait_recv()
     mix(1)
     mix(0)
@@ -436,19 +449,21 @@
             if dx or dy:
                 wa(dx, dy).wait_send()
     for a in range(2):
-        a_out(a, 1, 0, True).wait_send()
-        a_out(a, 1, 0, False).wait_send()
-        a_out(a, 0, 0, False).wait_send()
-        for dy in (1, 3, 2):
-            a_out(a, 0, dy, True).wait_send()
-            a_out(a, 0, dy, False).wait_send()
-            a_on(a, dy, 0).wait_send()
-            a_on(a, dy, 1).wait_send()
+        for k, dy in ROUTE:
+            if k or dy:
+                a_out(a, k, dy, True).wait_send()
+            a_out(a, k, dy, False).wait_send()
     halo_sent(0)
 
     @pl.when(has_later)
     def _():
         t_halo(0).wait_send()
+        t_halo(1).wait_send()
+        far_1.wait_send()
+
+    @pl.when(has_relay)
+    def _():
+        far_2.wait_send()
 
     @pl.when(has_prev)
     def _():
@@ -479,8 +494,9 @@
             pltpu.VMEM((2, 2, 128, 128), BF16),
             pltpu.VMEM((2, 8, 2, 2, 128, 128), BF16),
             pltpu.VMEM((2, 128, 512), F32),
+            pltpu.VMEM((64, 256), BF16),
             dma(4), dma(4), dma(40), dma(40), dma(32), dma(2), dma(6), dma(9),
-            dma(16), dma(1), dma(32),
+            dma(16), dma(1), dma(32), dma(2),
         ],
         compiler_params=pltpu.CompilerParams(
             collective_id=0, has_side_effects=True, vmem_limit_bytes=56 * 2 ** 20),

time: 96.7 us -> 94.8 us (0.980)
  the two profiles are of different devices: /device:TPU:160 before, /device:TPU:135 now
where the time goes in v3:
time: 94.8 us; the launch traced here: 94.6 us
  Pallas kernels  92.9 us (98%)
  local copies, waits for them, and re-layouts  1.67 us (2%)
    pallas_call x1, Pallas kernels, per_device(): pl.pallas_call(kernel, out_shape=jax.ShapeDtypeStruct((256, 512), BF16),...  92.9 us

profile of v3, /device:TPU:135, one launch (start us, length us, event | category | flops | bytes accessed | tf_op | source)
XLA Modules:
  0.0 94.6 jit_solution(4154181582085029926)
XLA Ops:
  0.0 92.9 %tile_attention.1 = bf16[256,512]{1,0:T(8,128)(2,1)} custom-call(s32[2,3]{1,0:T(2,128)} %win.1, bf16[256,4096]{1,0:T(8,128)(2,1)} %tok_in.1, bf16[3,64,256]{2,1,0:T(8,128)(2,1)} %w_in.1, bf16[64,256]{1,0:T(8,128)(2,1)} %bitcast.1), custom_call_target="tpu_custom_call" | custom-call | tf_op jit(solution)/shard_map/tile_attention/pallas_call | solution.py:478
  92.9 1.7 %copy.6 = bf16[256,512]{1,0:T(8,128)(2,1)} copy(bf16[256,512]{1,0:T(8,128)(2,1)} %tile_attention.1) | data formatting | bytes 524288

commit v4 on v3

--- a/solution.py
+++ b/solution.py
@@ -222,11 +222,11 @@
     FRAMES = (pl.ds(2, 2), pl.ds(1, 1), pl.ds(0, 1))
 
     def t_halo(f):
-        grp = MIDG if f else pl.ds(1, 3)
+        grp = MIDG if f else pl.ds(1, 2)
         return rc(kv.at[2 + f, grp, OWN, :], kv.at[f, grp, OWN, :], s_t, f, later)
 
-    far_1 = rc(kv.at[2, 4, OWN, :], relay, s_far, 0, six_down)
-    far_2 = rc(relay, kv.at[0, 4, OWN, :], s_far, 1, six_down)
+    far_1 = rc(kv.at[2, pl.ds(3, 2), OWN, :], relay, s_far, 0, six_down)
+    far_2 = rc(relay, kv.at[0, pl.ds(3, 2), OWN, :], s_far, 1, six_down)
     has_relay = (z + 6) % NZ < 12
 
     def h_down(i):
@@ -494,7 +494,7 @@
             pltpu.VMEM((2, 2, 128, 128), BF16),
             pltpu.VMEM((2, 8, 2, 2, 128, 128), BF16),
             pltpu.VMEM((2, 128, 512), F32),
-            pltpu.VMEM((64, 256), BF16),
+            pltpu.VMEM((2, 64, 256), BF16),
             dma(4), dma(4), dma(40), dma(40), dma(32), dma(2), dma(6), dma(9),
             dma(16), dma(1), dma(32), dma(2),
         ],

time: 94.8 us -> 91.6 us (0.966)
  the two profiles are of different devices: /device:TPU:135 before, /device:TPU:160 now
where the time goes in v4:
time: 91.6 us; the launch traced here: 91.2 us
  Pallas kernels  89.5 us (98%)
  local copies, waits for them, and re-layouts  1.67 us (2%)
    pallas_call x1, Pallas kernels, per_device(): pl.pallas_call(kernel, out_shape=jax.ShapeDtypeStruct((256, 512), BF16),...  89.5 us

profile of v4, /device:TPU:160, one launch (start us, length us, event | category | flops | bytes accessed | tf_op | source)
XLA Modules:
  0.0 91.2 jit_solution(17222175135909500372)
XLA Ops:
  0.0 89.5 %tile_attention.1 = bf16[256,512]{1,0:T(8,128)(2,1)} custom-call(s32[2,3]{1,0:T(2,128)} %win.1, bf16[256,4096]{1,0:T(8,128)(2,1)} %tok_in.1, bf16[3,64,256]{2,1,0:T(8,128)(2,1)} %w_in.1, bf16[64,256]{1,0:T(8,128)(2,1)} %bitcast.1), custom_call_target="tpu_custom_call" | custom-call | tf_op jit(solution)/shard_map/tile_attention/pallas_call | solution.py:478
  89.5 1.7 %copy.6 = bf16[256,512]{1,0:T(8,128)(2,1)} copy(bf16[256,512]{1,0:T(8,128)(2,1)} %tile_attention.1) | data formatting | bytes 524288

commit v5 on v4

--- a/solution.py
+++ b/solution.py
@@ -206,14 +206,6 @@
     def unit(p):
         return p * lax.rsqrt(jnp.mean(p * p, axis=-1, keepdims=True) + 1e-06)
 
-    for tw in range(2):
-        for a in range(2):
-            at_rows = pl.ds(tw * 256 + a * 128, 128)
-            both = jnp.concatenate([unit(acc[at_rows, 128:256]), acc[at_rows, 256:384]], axis=1)
-            both = both.reshape(8, 2, 8, 256)
-            for g in range(2):
-                kv[2 + a, 1 + tw * 2 + g, 32:96, :] = both[:, g].reshape(64, 256).astype(BF16)
-
     edge_out = 4 - 3 * xl
     edge_in = 5 * xl
     OWN, TOP, BOT = pl.ds(32, 64), pl.ds(0, 32), pl.ds(96, 32)
@@ -285,10 +277,24 @@
             h_up(i).wait_send()
             x_up(i).wait_send()
 
+    def place(a):
+        for tw in range(2):
+            at_rows = pl.ds(tw * 256 + a * 128, 128)
+            both = jnp.concatenate([unit(acc[at_rows, 128:256]), acc[at_rows, 256:384]], axis=1)
+            both = both.reshape(8, 2, 8, 256)
+            for g in range(2):
+                kv[2 + a, 1 + tw * 2 + g, 32:96, :] = both[:, g].reshape(64, 256).astype(BF16)
+
+    place(1)
+
     @pl.when(has_later)
     def _():
+        t_halo(1).start()
+    place(0)
+
+    @pl.when(has_later)
+    def _():
         far_1.start()
-        t_halo(1).start()
     halo_start(0)
 
     for ch in (2, 3, 4):

time: 91.6 us -> 92.3 us (level)
  no operation moved by 1% of the time
where the time goes in v5:
time: 92.3 us; the launch traced here: 91.5 us
  Pallas kernels  89.9 us (97%)
  local copies, waits for them, and re-layouts  1.67 us (2%)
    pallas_call x1, Pallas kernels, per_device(): pl.pallas_call(kernel, out_shape=jax.ShapeDtypeStruct((256, 512), BF16),...  89.9 us

profile of v5, /device:TPU:160, one launch (start us, length us, event | category | flops | bytes accessed | tf_op | source)
XLA Modules:
  0.0 91.5 jit_solution(15609447018140013050)
XLA Ops:
  0.0 89.9 %tile_attention.1 = bf16[256,512]{1,0:T(8,128)(2,1)} custom-call(s32[2,3]{1,0:T(2,128)} %win.1, bf16[256,4096]{1,0:T(8,128)(2,1)} %tok_in.1, bf16[3,64,256]{2,1,0:T(8,128)(2,1)} %w_in.1, bf16[64,256]{1,0:T(8,128)(2,1)} %bitcast.1), custom_call_target="tpu_custom_call" | custom-call | tf_op jit(solution)/shard_map/tile_attention/pallas_call | solution.py:484
  89.9 1.7 %copy.6 = bf16[256,512]{1,0:T(8,128)(2,1)} copy(bf16[256,512]{1,0:T(8,128)(2,1)} %tile_attention.1) | data formatting | bytes 524288
